TPU v7x, 512 devices: a whole 4x8x8 slice. The times are simulated.
512 devices in a mesh: row: 64 (over y, z_lo, core), col: 8 (over z_hi, x).
Axes of the slice: x: 4, y: 8, z: 8 (z_hi: 2, z_lo: 4; z = z_hi * 4 + z_lo), core: 2. Of those that a mesh axis runs over, the one named last changes fastest.
Arguments:
- telemetry: float32 [8, 2048, 64], P('col', 'row'), may hold values from -6 to 6
- target: int32 [8, 2048], P('col', 'row'), may hold values from 0 to 8191, as said below
- counts: int32 [8, 64], P('col', 'row'), may hold values from 0 to 32, as said below
- lengthscale: float32 [64], replicated, may hold values from 2 to 8
- nugget: float32 [8192], P('row'), may hold values from 0.1 to 1
Outputs:
- schur: float32 [8192, 8, 1024], P('row', 'col')
- lower_col: float32 [8192, 1024], P('row')
Inputs may be any that keep to these rules, and one draw needn't show every extreme that they name: `target`: the first counts slots of each device hold distinct location indices, and over all devices every location appears exactly once among them; later slots hold arbitrary indices. The used slots of device (c, r) name only locations of row blocks (r - d) mod 64 with 0 <= d < 16, at most 2 locations of any one row block, and exactly 2 for every block they name. `counts`: Even; 32 on some device of every index of col; the total over all devices is 8192.
All inputs are finite; a program needn't handle non-finite values.
Results may differ from a plain program's by a relative error of at most 0.0003.
Values sent between devices are 32-bit elements; how exact they have to be, the bound alone decides.
A program may use at most 128 MiB of HBM per device.

v0:
```python
import functools

import jax
import jax.numpy as jnp
from jax import lax
from jax.experimental import pallas as pl
from jax.experimental.pallas import tpu as pltpu
from jax.sharding import PartitionSpec as P

F = 64
PB = 1024
RB = 128
NR = 64
NC = 8
SL = 16
WIN = 16
SLOTS = 32
HI = lax.Precision.HIGHEST
MESH = pl.DeviceIdType.MESH

root_three = 1.7320508075688772


def hdot(a, b):
    return jnp.dot(a, b, precision=HI, preferred_element_type=jnp.float32)


def exchange_kernel(
    tel_ref, tgt_ref, cnt_ref, nug_ref,
    blk_ref, col_ref, pan_ref, pnug_ref,
    out1, in1, comp, gath, mine, nugtile,
    s1, r1, s2, r2, s3, r3, s4, r4, s5, r5,
):
    r = lax.axis_index("row")
    c = lax.axis_index("col")

    def at_row(peer):
        return (peer, c)

    def at_col(peer):
        return (r, peer)

    barrier = pltpu.get_barrier_semaphore()

    def greet_row(i, carry):
        pl.semaphore_signal(
            barrier, inc=1, device_id=at_row(lax.rem(r + i, NR)), device_id_type=MESH
        )
        return carry

    def greet_col(i, carry):
        pl.semaphore_signal(
            barrier, inc=1, device_id=at_col(lax.rem(c + i, NC)), device_id_type=MESH
        )
        return carry

    lax.fori_loop(1, NR, greet_row, 0)
    lax.fori_loop(1, NC, greet_col, 0)

    tel = tel_ref[0]
    t_row = tgt_ref[...]
    sub = lax.broadcasted_iota(jnp.int32, (SLOTS, SLOTS), 0)
    lane = lax.broadcasted_iota(jnp.int32, (SLOTS, SLOTS), 1)
    t_mat = jnp.broadcast_to(t_row, (SLOTS, SLOTS))
    t_col = jnp.sum(jnp.where(sub == lane, t_mat, 0), axis=1, keepdims=True)
    zone_row = lax.shift_right_logical(t_row, 7)
    zone_col = lax.shift_right_logical(t_col, 7)
    filled = cnt_ref[...]
    earlier = (zone_col == zone_row) & (sub < filled) & (sub < lane)
    position = jnp.sum(earlier.astype(jnp.int32), axis=0, keepdims=True)
    offset = jnp.bitwise_and(r - zone_row + NR, NR - 1)
    used = (lane[0:1] < filled) & (position < 2) & (offset < WIN)
    slot = jnp.where(used, offset * 2 + position, -1)
    place = jnp.bitwise_and(t_row, RB - 1).astype(jnp.float32)
    dist = lax.broadcasted_iota(jnp.int32, (WIN, SLOTS), 0) * 2
    pick0 = dist == slot
    pick1 = dist + 1 == slot
    feat0 = hdot(pick0.astype(jnp.float32), tel)
    feat1 = hdot(pick1.astype(jnp.float32), tel)
    place0 = jnp.max(jnp.where(pick0, place, -1.0), axis=1, keepdims=True)
    place1 = jnp.max(jnp.where(pick1, place, -1.0), axis=1, keepdims=True)
    feats = jnp.concatenate([feat0, feat1], axis=1)
    lane_w = lax.broadcasted_iota(jnp.int32, (WIN, 128), 1)
    places = jnp.where(lane_w < F, place0, place1)
    tile_row = lax.broadcasted_iota(jnp.int32, (8, 128), 0)
    for d in range(WIN):
        out1[d] = jnp.where(
            tile_row == d % 8,
            feats[d : d + 1],
            jnp.where(tile_row == (d + 4) % 8, places[d : d + 1], 0.0),
        )
    in1[0] = out1[0]
    nugtile[...] = jnp.broadcast_to(nug_ref[...], (8, 128))

    pl.semaphore_wait(barrier, NR - 1 + NC - 1)

    def step1(d):
        return pltpu.make_async_remote_copy(
            src_ref=out1.at[d], dst_ref=in1.at[d], send_sem=s1, recv_sem=r1,
            device_id=at_row(jnp.bitwise_and(r - d + NR, NR - 1)), device_id_type=MESH,
        )

    def start1(d, carry):
        step1(d).start()
        return carry

    lax.fori_loop(1, WIN, start1, 0)

    def drain(ref, sem):
        pltpu.make_async_copy(ref, ref, sem).wait()

    def step5(i, slot_id):
        return pltpu.make_async_remote_copy(
            src_ref=nugtile, dst_ref=pnug_ref.at[slot_id], send_sem=s5, recv_sem=r5,
            device_id=at_row(jnp.bitwise_and(r + i, NR - 1)), device_id_type=MESH,
        )

    drain(in1.at[pl.ds(1, WIN - 1)], r1)
    for half in range(2):
        feat_rows = jnp.zeros((8, 128), jnp.float32)
        place_rows = jnp.zeros((8, 128), jnp.float32)
        for d in range(8):
            got = in1[8 * half + d]
            feat_rows = jnp.where(tile_row == d, got, feat_rows)
            place_rows = jnp.where(tile_row == (d + 4) % 8, got, place_rows)
        comp[8 * half : 8 * half + 8, :] = feat_rows
        comp[WIN + 8 * half : WIN + 8 * half + 8, :] = pltpu.roll(place_rows, 4, 0)

    def step2(i, slot_id):
        return pltpu.make_async_remote_copy(
            src_ref=comp, dst_ref=gath.at[slot_id], send_sem=s2, recv_sem=r2,
            device_id=at_col(jnp.bitwise_and(c + i, NC - 1)), device_id_type=MESH,
        )

    for i in range(1, NC):
        step2(i, c).start()
    gath[c] = comp[...]

    @pl.when(r < NC)
    def _():
        def start5(i, carry):
            step5(i, r).start()
            return carry

        lax.fori_loop(1, NR, start5, 0)
        pnug_ref[r] = nugtile[...]

    drain(gath.at[pl.ds(1, NC - 1)], r2)

    all_feats = gath[:, 0:WIN, :].reshape(NC * WIN, 128)
    all_places = gath[:, WIN : 2 * WIN, :].reshape(NC * WIN, 128)
    hi_p, mid_p, low_p = parts(all_feats)
    stack = jnp.concatenate([hi_p, mid_p, low_p], axis=0)

    def placed(first, count):
        spot = first + lax.broadcasted_iota(jnp.int32, (NC * WIN, count), 1)
        spot = spot.astype(jnp.float32)
        put0 = (all_places[:, 0:1] == spot).astype(jnp.bfloat16)
        put1 = (all_places[:, F : F + 1] == spot).astype(jnp.bfloat16)
        rows0 = stacked(jnp.concatenate([put0] * 3, axis=0), stack)
        rows1 = stacked(jnp.concatenate([put1] * 3, axis=0), stack)
        return rows0[:, 0:F] + rows1[:, F : 2 * F]

    group = placed(c * SL, SL)
    mine[:, 0:F] = group[0:8]
    mine[:, F : 2 * F] = group[8:SL]

    late = (r >= NC).astype(jnp.int32)

    def step3(i, slot_id):
        return pltpu.make_async_remote_copy(
            src_ref=mine, dst_ref=col_ref.at[slot_id], send_sem=s3, recv_sem=r3.at[late],
            device_id=at_row(jnp.bitwise_and(r + i, NR - 1)), device_id_type=MESH,
        )

    def start3(i, carry):
        step3(i, r).start()
        return carry

    lax.fori_loop(1, NR, start3, 0)
    col_ref[r] = mine[...]
    blk_ref[...] = placed(0, RB)

    @pl.when(r < NC)
    def _():
        drain(col_ref.at[pl.ds(0, NC - 1)], r3.at[0])

    @pl.when(r >= NC)
    def _():
        drain(col_ref.at[pl.ds(0, NC)], r3.at[0])

    def step4(i, slot_id):
        return pltpu.make_async_remote_copy(
            src_ref=col_ref.at[pl.ds(0, NC)], dst_ref=pan_ref.at[slot_id], send_sem=s4,
            recv_sem=r4,
            device_id=at_col(jnp.bitwise_and(c + i, NC - 1)), device_id_type=MESH,
        )

    for i in range(1, NC):
        step4(i, c).start()
    pan_ref[c] = col_ref[0:NC]

    @pl.when(r < NC)
    def _():
        drain(col_ref.at[pl.ds(NC, NR - NC)], r3.at[1])
        drain(pnug_ref.at[pl.ds(0, NC - 1)], r5)

    @pl.when(r >= NC)
    def _():
        drain(col_ref.at[pl.ds(NC, NR - NC - 1)], r3.at[1])
        drain(pnug_ref, r5)

    drain(in1.at[pl.ds(1, WIN - 1)], s1)
    drain(gath.at[pl.ds(1, NC - 1)], s2)
    drain(col_ref.at[pl.ds(1, NR - 1)], s3)
    drain(pan_ref.at[pl.ds(1, NC - 1)], r4)
    drain(pan_ref.at[pl.ds(1, NC - 1)], s4)

    @pl.when(r < NC)
    def _():
        drain(col_ref.at[pl.ds(1, NR - 1)], s5)


def exchange(telemetry, target, counts, nugget):
    dma = pltpu.SemaphoreType.DMA
    vmem = pl.BlockSpec(memory_space=pltpu.VMEM)
    f32 = jnp.float32
    return pl.pallas_call(
        exchange_kernel,
        out_shape=(
            jax.ShapeDtypeStruct((RB, F), f32),
            jax.ShapeDtypeStruct((NR, 8, 128), f32),
            jax.ShapeDtypeStruct((NC, NC, 8, 128), f32),
            jax.ShapeDtypeStruct((NC, 8, 128), f32),
        ),
        in_specs=[vmem] * 4,
        out_specs=(vmem,) * 4,
        scratch_shapes=[
            pltpu.VMEM((WIN, 8, 128), f32),
            pltpu.VMEM((WIN, 8, 128), f32),
            pltpu.VMEM((2 * WIN, 128), f32),
            pltpu.VMEM((NC, 2 * WIN, 128), f32),
            pltpu.VMEM((8, 128), f32),
            pltpu.VMEM((8, 128), f32),
            dma(()), dma(()), dma(()), dma(()), dma(()), dma((2,)),
            dma(()), dma(()), dma(()), dma(()),
        ],
        compiler_params=pltpu.CompilerParams(
            collective_id=0, has_side_effects=True, vmem_limit_bytes=32 * 1024 * 1024
        ),
        name="exchange",
    )(telemetry, target, counts, nugget.reshape(1, RB))


def sublanes(x, i):
    return jnp.broadcast_to(x[i : i + 1, :], (8, RB))


def lanes(x, j):
    return lax.gather(
        x,
        jnp.full((8, RB, 1), j, jnp.int32),
        lax.GatherDimensionNumbers(
            offset_dims=(), collapsed_slice_dims=(1,), start_index_map=(1,),
            operand_batching_dims=(0,), start_indices_batching_dims=(0,),
        ),
        slice_sizes=(1, 1),
        mode=lax.GatherScatterMode.PROMISE_IN_BOUNDS,
    )


def parts(x):
    f32 = jnp.float32
    hi = x.astype(jnp.bfloat16)
    rest = x - hi.astype(f32)
    mid = rest.astype(jnp.bfloat16)
    low = (rest - mid.astype(f32)).astype(jnp.bfloat16)
    return hi, mid, low


def left_stack(p, axis=0):
    hi, mid, low = p
    return jnp.concatenate([hi, hi, hi, mid, mid, low], axis=axis)


def right_stack(p):
    hi, mid, low = p
    return jnp.concatenate([hi, mid, low, hi, mid, hi], axis=0)


def left_short(p):
    return jnp.concatenate([p[0], p[0], p[1]], axis=0)


def right_short(p):
    return jnp.concatenate([p[0], p[1], p[0]], axis=0)


def stacked(left, right, over=0):
    return lax.dot_general(
        left, right, (((over,), (0,)), ((), ())), preferred_element_type=jnp.float32
    )


def gram(u):
    f32 = jnp.float32
    hi = u.astype(jnp.bfloat16).astype(f32)
    rest = u - hi
    mid = rest.astype(jnp.bfloat16).astype(f32)
    low = rest - mid
    left = jnp.concatenate([hi, hi, hi, mid, mid, low], axis=0).astype(jnp.bfloat16)
    right = jnp.concatenate([hi, mid, low, hi, mid, hi], axis=0).astype(jnp.bfloat16)
    return stacked(left, right)


AHEAD = 3


def factor_block(groups, fill):
    groups = list(groups)
    count = len(groups)
    sub = lax.broadcasted_iota(jnp.int32, (8, RB), 0)
    lane = lax.broadcasted_iota(jnp.int32, (8, RB), 1)
    for g in range(count):
        first = 8 * g
        near = list(range(g, min(count, g + AHEAD)))
        cols = {h: [lanes(groups[h], first + k) for k in range(8)] for h in near}
        in_panel = (lane >= first) & (lane < first + 8)
        one = (lane - first == sub).astype(jnp.float32)
        for h in range(g, count):
            groups[h] = jnp.where(in_panel, one if h == g else 0.0, groups[h])
        pivots = jnp.ones((8, RB), jnp.float32)
        small = [[sublanes(cols[g][k], i) if k >= i else None for k in range(8)] for i in range(8)]
        for i in range(8):
            fill(8 * g + i)
            inv = pl.reciprocal(small[i][i], approx=True)
            inv = inv * (2.0 - small[i][i] * inv)
            pivots = jnp.where(sub == i, small[i][i], pivots)
            row = sublanes(groups[g], i)
            for j in range(i + 1, 8):
                scale = small[i][j] * inv
                for k in range(j, 8):
                    small[j][k] = small[j][k] - scale * small[i][k]
            for h in near:
                step = cols[h][i] * inv
                if h == g:
                    step = jnp.where(sub > i, step, 0.0)
                for k in range(i + 1, 8):
                    cols[h][k] = cols[h][k] - step * small[i][k]
                if h != g or i < 7:
                    groups[h] = groups[h] - step * row
        done = groups[g] * lax.rsqrt(pivots)
        groups[g] = done
        if g + AHEAD < count:
            product = gram(done)
            for h in range(g + AHEAD, count):
                groups[h] = groups[h] - product[8 * h : 8 * h + 8, :]
    return groups


def matern(left, left_sq, right, right_sq):
    squared = left_sq + right_sq - 2.0 * stacked(left, right)
    scaled = root_three * jnp.sqrt(jnp.maximum(squared, 0.0))
    return (1.0 + scaled) * jnp.exp(-scaled)


def spread(jobs, slots):
    def fill(slot):
        for job in jobs[slot * len(jobs) // slots : (slot + 1) * len(jobs) // slots]:
            job()

    return fill


WIDTH = PB + RB
LAST = PB - RB


def factor_kernel(
    where_ref, blk_ref, col_ref, pan_ref, pnug_ref, nug_ref, len_ref,
    schur_ref, lower_ref,
    pts, cpts, nugs, sq_l, sq_r, sq_c, p_l, p_r, c_r, big, across, weights, u_ref, partial,
):
    r = where_ref[0]
    c = where_ref[1]
    inv = 1.0 / len_ref[...]
    pts[PB:, :] = blk_ref[...] * inv
    for rb in range(NC):
        nugs[:, rb * RB : (rb + 1) * RB] = pnug_ref[rb]
        for cc in range(NC):
            at = rb * RB + cc * SL
            both = pan_ref[cc, rb]
            pts[at : at + 8, :] = both[:, 0:F] * inv
            pts[at + 8 : at + SL, :] = both[:, F : 2 * F] * inv
    for rb in range(NR):
        both = col_ref[rb]
        cpts[rb * SL : rb * SL + 8, :] = both[:, 0:F] * inv
        cpts[rb * SL + 8 : rb * SL + SL, :] = both[:, F : 2 * F] * inv
    for i in range(NC + 1):
        at = i * RB
        block = pts[at : at + RB, :]
        turned = block.T
        sq_l[at : at + RB, :] = jnp.sum(block * block, axis=1, keepdims=True)
        sq_r[:, at : at + RB] = jnp.sum(turned * turned, axis=0, keepdims=True)
        p = parts(turned)
        p_l[:, at : at + RB] = left_stack(p)
        p_r[:, at : at + RB] = right_stack(p)
    for i in range(NC):
        at = i * RB
        turned = cpts[at : at + RB, :].T
        sq_c[:, at : at + RB] = jnp.sum(turned * turned, axis=0, keepdims=True)
        c_r[:, at : at + RB] = right_stack(parts(turned))

    eye = lax.broadcasted_iota(jnp.int32, (RB, RB), 0) == lax.broadcasted_iota(
        jnp.int32, (RB, RB), 1
    )
    low = lax.broadcasted_iota(jnp.int32, (RB, RB), 0) >= lax.broadcasted_iota(
        jnp.int32, (RB, RB), 1
    )
    sub = lax.broadcasted_iota(jnp.int32, (RB, 1), 0)

    def column_ids(start, width):
        n = start + lax.broadcasted_iota(jnp.int32, (1, width), 1)
        return lax.shift_right_logical(n, 4) * RB + c * SL + jnp.bitwise_and(n, SL - 1)

    def panel_job(i, lo, hi):
        def job():
            at = i * RB
            block = matern(
                p_l[:, at : at + RB], sq_l[at : at + RB, :], p_r[:, lo:hi], sq_r[:, lo:hi]
            )
            if lo == at:
                block = block + jnp.where(eye, nugs[0:1, at : at + RB], 0.0)
            if lo == PB:
                same = jnp.where(r == i, 1.0, 0.0)
                block = block + same * jnp.where(eye, nugs[0:1, at : at + RB], 0.0)
            big[at : at + RB, lo:hi] = block

        return job

    def across_job(i, lo, hi):
        def job():
            at = i * RB
            block = matern(
                p_l[:, at : at + RB], sq_l[at : at + RB, :], c_r[:, lo:hi], sq_c[:, lo:hi]
            )
            if lo < RB:
                nug_col = jnp.sum(
                    jnp.where(eye, nugs[0:1, at : at + RB], 0.0), axis=1, keepdims=True
                )
                block = block + jnp.where(at + sub == column_ids(lo, hi - lo), nug_col, 0.0)
            for q, part in enumerate(parts(block)[0:2]):
                across[q, at : at + RB, lo:hi] = part

        return job

    def keep(half, lo, hi, value):
        hi_p, mid_p, low_p = parts(value)
        u_ref[half, 0, :, lo:hi] = hi_p
        u_ref[half, 1, :, lo:hi] = mid_p
        u_ref[half, 2, :, lo:hi] = low_p

    def kept(half, lo, hi):
        return tuple(u_ref[half, q, :, lo:hi] for q in range(3))

    def row_job(k, left, lo, hi):
        def job():
            at = k * RB
            value = stacked(left, right_stack(parts(big[at : at + RB, lo:hi])), 1)
            big[at : at + RB, lo:hi] = value
            keep(k % 2, lo, hi, value)

        return job

    def update_job(k, i, lo, hi):
        def job():
            at = i * RB
            change = stacked(
                left_stack(kept(k % 2, at, at + RB)), right_stack(kept(k % 2, lo, hi))
            )
            if lo == k * RB:
                big[at : at + RB, lo:hi] = -change
            else:
                big[at : at + RB, lo:hi] = big[at : at + RB, lo:hi] - change

        return job

    def weight_job(j):
        def job():
            at = j * RB
            weights[at : at + RB, :] = stacked(
                left_short(parts(big[at:LAST, at : at + RB])),
                right_short(parts(big[at:LAST, PB:])),
            )

        return job

    def partial_job(lo, hi):
        def job():
            nug_own = jnp.sum(jnp.where(eye, nug_ref[...], 0.0), axis=1, keepdims=True)
            partial[:, lo:hi] = matern(
                p_l[:, PB:], sq_l[PB:, :], c_r[:, lo:hi], sq_c[:, lo:hi]
            ) + jnp.where(r * RB + sub == column_ids(lo, hi - lo), nug_own, 0.0)

        return job

    def lower_job(j):
        def job():
            at = j * RB
            lower_ref[:, at : at + RB] = big[at : at + RB, PB:].T

        return job

    def pieces(lo, hi, size=2 * RB):
        return [(x, min(hi, x + size)) for x in range(lo, hi, size)]

    panel_job(0, 0, RB)()
    jobs = []
    for i in range(NC):
        spans = pieces((i if i else 1) * RB, PB) if i == 0 else [(i * RB, (i + 1) * RB)]
        if i:
            spans = spans + pieces((i + 1) * RB, PB)
        jobs += [panel_job(i, lo, hi) for lo, hi in spans + [(PB, WIDTH)]]
    extra = {2: (0, 2), 3: (2, 9), 4: (9, 17), 5: (17, 25), 6: (25, 32)}
    slices = [(i, lo, hi) for i in range(NC) for lo, hi in pieces(0, PB)]
    square = big[0:RB, 0:RB]
    for k in range(NC):
        at = k * RB
        if k in extra:
            jobs += [across_job(*x) for x in slices[extra[k][0] : extra[k][1]]]
        if k == NC - 1:
            jobs += [lower_job(j) for j in range(NC - 1)]
            jobs += [partial_job(lo, hi) for lo, hi in pieces(0, PB)]
            jobs += [weight_job(j) for j in range(NC - 1)]
        groups = factor_block([square[h : h + 8, :] for h in range(0, RB, 8)], spread(jobs, RB))
        inverse = jnp.where(low, jnp.concatenate(groups, axis=0), 0.0)
        left = left_stack(parts(inverse), axis=1)
        nxt = at + RB
        if k < NC - 1:
            beside = stacked(left, right_stack(parts(big[at:nxt, nxt : nxt + RB])), 1)
            p = parts(beside)
            square = big[nxt : nxt + RB, nxt : nxt + RB] - stacked(left_stack(p), right_stack(p))
            keep(k % 2, nxt, nxt + RB, beside)
        big[at:nxt, at:nxt] = inverse
        keep(k % 2, at, nxt, inverse)
        jobs = [row_job(k, left, lo, hi) for lo, hi in pieces(0, at)]
        jobs += [row_job(k, left, lo, hi) for lo, hi in pieces(min(nxt + RB, PB), WIDTH)]
        for i in range(k + 1, NC):
            start = (i if i > k + 1 else i + 1) * RB
            spans = pieces(0, at) + [(at, nxt)] + pieces(start, WIDTH)
            jobs += [update_job(k, i, lo, hi) for lo, hi in spans]
    for job in jobs:
        job()
    lower_job(NC - 1)()
    change = stacked(
        left_short(parts(big[LAST:, 0:PB])), right_short(parts(big[LAST:, PB:]))
    )
    w_left = left_short(parts(jnp.concatenate([weights[0:LAST, :] + change[0:LAST], change[LAST:]], axis=0)))
    for lo, hi in pieces(0, PB):
        hi_p, mid_p = across[0, :, lo:hi], across[1, :, lo:hi]
        value = partial[:, lo:hi] - stacked(w_left, right_short((hi_p, mid_p)))
        for q in range(lo // RB, hi // RB):
            schur_ref[:, q, :] = value[:, q * RB - lo : (q + 1) * RB - lo]


def factor_and_update(where, blk, col, pan, pnug, nugget, lengthscale):
    vmem = pl.BlockSpec(memory_space=pltpu.VMEM)
    f32 = jnp.float32
    return pl.pallas_call(
        factor_kernel,
        out_shape=(
            jax.ShapeDtypeStruct((RB, NC, RB), f32),
            jax.ShapeDtypeStruct((RB, PB), f32),
        ),
        in_specs=[pl.BlockSpec(memory_space=pltpu.SMEM)] + [vmem] * 6,
        out_specs=(vmem, vmem),
        scratch_shapes=[
            pltpu.VMEM((WIDTH, F), f32),
            pltpu.VMEM((PB, F), f32),
            pltpu.VMEM((8, PB), f32),
            pltpu.VMEM((WIDTH, 1), f32),
            pltpu.VMEM((1, WIDTH), f32),
            pltpu.VMEM((1, PB), f32),
            pltpu.VMEM((6 * F, WIDTH), jnp.bfloat16),
            pltpu.VMEM((6 * F, WIDTH), jnp.bfloat16),
            pltpu.VMEM((6 * F, PB), jnp.bfloat16),
            pltpu.VMEM((PB, WIDTH), f32),
            pltpu.VMEM((2, PB, PB), jnp.bfloat16),
            pltpu.VMEM((PB, RB), f32),
            pltpu.VMEM((2, 3, RB, WIDTH), jnp.bfloat16),
            pltpu.VMEM((RB, PB), f32),
        ],
        compiler_params=pltpu.CompilerParams(vmem_limit_bytes=48 * 1024 * 1024),
        name="factor",
    )(where, blk, col, pan, pnug, nugget.reshape(1, RB), lengthscale.reshape(1, F))


def body(telemetry, target, counts, lengthscale, nugget):
    block_pts, col_packed, pan_packed, pnug = exchange(telemetry, target, counts, nugget)
    where = jnp.stack([lax.axis_index("row"), lax.axis_index("col")]).astype(jnp.int32)
    schur_tile, row_lower = factor_and_update(
        where, block_pts, col_packed, pan_packed, pnug, nugget, lengthscale
    )
    return (schur_tile.reshape(RB, 1, PB), row_lower)


def solution(mesh):
    in_specs = (P("col", "row", None), P("col", "row"), P("col", "row"), P(), P("row"))
    out_specs = (P("row", "col", None), P("row", None))
    return jax.shard_map(body, mesh=mesh, in_specs=in_specs, out_specs=out_specs, check_vma=False)
```

profile of v0, /device:TPU:4, one launch (start us, length us, event | category | flops | bytes accessed | tf_op | source)
XLA Modules:
  0.0 86.3 jit_solution(18385771988944428093)
XLA Ops:
  0.6 0.0 copy-start
  1.3 0.1 pad_add_fusion.where_ref
  1.4 0.0 copy-start.1
  1.4 0.0 copy-start.2
  1.4 0.0 copy-done
  1.4 0.6 copy-done.1
  2.0 0.0 copy-done.2
  2.0 41.5 %exchange.1 = (f32[128,64]{1,0:T(8,128)S(1)}, f32[64,8,128]{2,1,0:T(8,128)S(1)}, f32[8,8,8,128]{3,2,1,0:T(8,128)S(1)}, f32[8,8,128]{2,1,0:T(8,128)S(1)}) custom-call(f32[1,32,64]{2,1,0:T(8,128)S(1)} %copy-done, s32[1,32]{1,0:T(1,128)S(1)} %copy-done.2, s32[1,1]{1,0:T(1,128)S(6)} %copy.8.cnt_ref, f32[1,128]{1,0:T(1,128)S(1)} %bitcast.5), custom_call_target="tpu_custom_call" | custom-call | tf_op jit(solution)/shard_map/exchange/pallas_call | solution.py:228
  43.6 0.0 copy-start.3
  43.6 0.6 copy-done.3
  44.2 42.0 %factor.1 = (f32[128,8,128]{2,1,0:T(8,128)}, f32[128,1024]{1,0:T(8,128)}) custom-call(s32[2]{0:T(128)S(1)} %pad_add_fusion.where_ref, f32[128,64]{1,0:T(8,128)S(1)} %get-tuple-element.8.blk_ref, f32[64,8,128]{2,1,0:T(8,128)S(1)} %get-tuple-element.9.col_ref, f32[8,8,8,128]{3,2,1,0:T(8,128)S(1)} %get-tuple-element.10.pan_ref, ...), custom_call_target="tpu_custom_call" | custom-call | tf_op jit(solution)/shard_map/factor/pallas_call | solution.py:569
Async XLA Ops:
  0.6 0.8 copy-start
  1.4 0.7 copy-start.1
  1.4 0.7 copy-start.2
  43.6 0.7 copy-start.3
where the time goes:
time: 86.5 us; the launch traced here: 86.3 us
  Pallas kernels  83.6 us (97%)
  local copies, waits for them, and re-layouts  1.32 us (2%)
  between operations  1.32 us (2%)
    pallas_call x1, Pallas kernels, factor_and_update(): pl.pallas_call(factor_kernel, out_shape=(jax.ShapeDtypeStruct((RB, NC, RB...  42 us
    pallas_call x1, Pallas kernels, exchange(): pl.pallas_call(exchange_kernel, out_shape=(jax.ShapeDtypeStruct((RB, F),...  41.5 us

commit v1 on v0

--- a/solution.py
+++ b/solution.py
@@ -26,7 +26,7 @@
 
 
 def exchange_kernel(
-    tel_ref, tgt_ref, cnt_ref, nug_ref,
+    tel_ref, tgt_ref, cnt_ref, nug_ref, len_ref,
     blk_ref, col_ref, pan_ref, pnug_ref,
     out1, in1, comp, gath, mine, nugtile,
     s1, r1, s2, r2, s3, r3, s4, r4, s5, r5,
@@ -57,7 +57,7 @@
     lax.fori_loop(1, NR, greet_row, 0)
     lax.fori_loop(1, NC, greet_col, 0)
 
-    tel = tel_ref[0]
+    tel = tel_ref[0] * (1.0 / len_ref[...])
     t_row = tgt_ref[...]
     sub = lax.broadcasted_iota(jnp.int32, (SLOTS, SLOTS), 0)
     lane = lax.broadcasted_iota(jnp.int32, (SLOTS, SLOTS), 1)
@@ -221,7 +221,7 @@
         drain(col_ref.at[pl.ds(1, NR - 1)], s5)
 
 
-def exchange(telemetry, target, counts, nugget):
+def exchange(telemetry, target, counts, nugget, lengthscale):
     dma = pltpu.SemaphoreType.DMA
     vmem = pl.BlockSpec(memory_space=pltpu.VMEM)
     f32 = jnp.float32
@@ -233,7 +233,7 @@
             jax.ShapeDtypeStruct((NC, NC, 8, 128), f32),
             jax.ShapeDtypeStruct((NC, 8, 128), f32),
         ),
-        in_specs=[vmem] * 4,
+        in_specs=[vmem] * 5,
         out_specs=(vmem,) * 4,
         scratch_shapes=[
             pltpu.VMEM((WIN, 8, 128), f32),
@@ -249,7 +249,7 @@
             collective_id=0, has_side_effects=True, vmem_limit_bytes=32 * 1024 * 1024
         ),
         name="exchange",
-    )(telemetry, target, counts, nugget.reshape(1, RB))
+    )(telemetry, target, counts, nugget.reshape(1, RB), lengthscale.reshape(1, F))
 
 
 def sublanes(x, i):
@@ -359,8 +359,8 @@
 
 
 def matern(left, left_sq, right, right_sq):
-    squared = left_sq + right_sq - 2.0 * stacked(left, right)
-    scaled = root_three * jnp.sqrt(jnp.maximum(squared, 0.0))
+    squared = jnp.maximum(left_sq + right_sq + stacked(left, right, 1), 1e-30)
+    scaled = squared * lax.rsqrt(squared)
     return (1.0 + scaled) * jnp.exp(-scaled)
 
 
@@ -377,39 +377,46 @@
 
 
 def factor_kernel(
-    where_ref, blk_ref, col_ref, pan_ref, pnug_ref, nug_ref, len_ref,
+    where_ref, blk_ref, col_ref, pan_ref, pnug_ref, nug_ref,
     schur_ref, lower_ref,
-    pts, cpts, nugs, sq_l, sq_r, sq_c, p_l, p_r, c_r, big, across, weights, u_ref, partial,
+    pts, cpts, nugs, sq_l, sq_r, sq_c, p_l, p_r, c_r, big, across, weights, u_ref, partial, l_ref,
 ):
     r = where_ref[0]
     c = where_ref[1]
-    inv = 1.0 / len_ref[...]
-    pts[PB:, :] = blk_ref[...] * inv
-    for rb in range(NC):
-        nugs[:, rb * RB : (rb + 1) * RB] = pnug_ref[rb]
-        for cc in range(NC):
-            at = rb * RB + cc * SL
-            both = pan_ref[cc, rb]
-            pts[at : at + 8, :] = both[:, 0:F] * inv
-            pts[at + 8 : at + SL, :] = both[:, F : 2 * F] * inv
-    for rb in range(NR):
-        both = col_ref[rb]
-        cpts[rb * SL : rb * SL + 8, :] = both[:, 0:F] * inv
-        cpts[rb * SL + 8 : rb * SL + SL, :] = both[:, F : 2 * F] * inv
-    for i in range(NC + 1):
-        at = i * RB
-        block = pts[at : at + RB, :]
-        turned = block.T
-        sq_l[at : at + RB, :] = jnp.sum(block * block, axis=1, keepdims=True)
-        sq_r[:, at : at + RB] = jnp.sum(turned * turned, axis=0, keepdims=True)
-        p = parts(turned)
-        p_l[:, at : at + RB] = left_stack(p)
-        p_r[:, at : at + RB] = right_stack(p)
-    for i in range(NC):
-        at = i * RB
-        turned = cpts[at : at + RB, :].T
-        sq_c[:, at : at + RB] = jnp.sum(turned * turned, axis=0, keepdims=True)
-        c_r[:, at : at + RB] = right_stack(parts(turned))
+
+    def prepare(i):
+        def job():
+            at = i * RB
+            if i == NC:
+                block = blk_ref[...]
+            else:
+                nugs[:, at : at + RB] = pnug_ref[i]
+                for cc in range(NC):
+                    both = pan_ref[cc, i]
+                    pts[at + cc * SL : at + cc * SL + 8, :] = both[:, 0:F]
+                    pts[at + cc * SL + 8 : at + cc * SL + SL, :] = both[:, F : 2 * F]
+                block = pts[at : at + RB, :]
+            turned = block.T
+            sq_l[at : at + RB, :] = 3.0 * jnp.sum(block * block, axis=1, keepdims=True)
+            sq_r[:, at : at + RB] = 3.0 * jnp.sum(turned * turned, axis=0, keepdims=True)
+            wide = left_stack(tuple(q.astype(jnp.float32) for q in parts(-6.0 * turned)))
+            p_l[at : at + RB, :] = wide.T.astype(jnp.bfloat16)
+            p_r[:, at : at + RB] = right_stack(parts(turned))
+
+        return job
+
+    def prepare_columns(i):
+        def job():
+            at = i * RB
+            for q in range(NC):
+                both = col_ref[i * NC + q]
+                cpts[at + q * SL : at + q * SL + 8, :] = both[:, 0:F]
+                cpts[at + q * SL + 8 : at + q * SL + SL, :] = both[:, F : 2 * F]
+            turned = cpts[at : at + RB, :].T
+            sq_c[:, at : at + RB] = 3.0 * jnp.sum(turned * turned, axis=0, keepdims=True)
+            c_r[:, at : at + RB] = right_stack(parts(turned))
+
+        return job
 
     eye = lax.broadcasted_iota(jnp.int32, (RB, RB), 0) == lax.broadcasted_iota(
         jnp.int32, (RB, RB), 1
@@ -427,7 +434,7 @@
         def job():
             at = i * RB
             block = matern(
-                p_l[:, at : at + RB], sq_l[at : at + RB, :], p_r[:, lo:hi], sq_r[:, lo:hi]
+                p_l[at : at + RB, :], sq_l[at : at + RB, :], p_r[:, lo:hi], sq_r[:, lo:hi]
             )
             if lo == at:
                 block = block + jnp.where(eye, nugs[0:1, at : at + RB], 0.0)
@@ -442,7 +449,7 @@
         def job():
             at = i * RB
             block = matern(
-                p_l[:, at : at + RB], sq_l[at : at + RB, :], c_r[:, lo:hi], sq_c[:, lo:hi]
+                p_l[at : at + RB, :], sq_l[at : at + RB, :], c_r[:, lo:hi], sq_c[:, lo:hi]
             )
             if lo < RB:
                 nug_col = jnp.sum(
@@ -454,7 +461,11 @@
 
         return job
 
-    def keep(half, lo, hi, value):
+    def keep(k, lo, hi, value):
+        half = k % 2
+        for x in range(max(lo, (k + 1) * RB), min(hi, PB), RB):
+            for q, part in enumerate(parts(value[:, x - lo : x - lo + RB].T)):
+                l_ref[half, q, x : x + RB, :] = part
         hi_p, mid_p, low_p = parts(value)
         u_ref[half, 0, :, lo:hi] = hi_p
         u_ref[half, 1, :, lo:hi] = mid_p
@@ -468,7 +479,7 @@
             at = k * RB
             value = stacked(left, right_stack(parts(big[at : at + RB, lo:hi])), 1)
             big[at : at + RB, lo:hi] = value
-            keep(k % 2, lo, hi, value)
+            keep(k, lo, hi, value)
 
         return job
 
@@ -476,7 +487,9 @@
         def job():
             at = i * RB
             change = stacked(
-                left_stack(kept(k % 2, at, at + RB)), right_stack(kept(k % 2, lo, hi))
+                left_stack(tuple(l_ref[k % 2, q, at : at + RB, :] for q in range(3)), axis=1),
+                right_stack(kept(k % 2, lo, hi)),
+                1,
             )
             if lo == k * RB:
                 big[at : at + RB, lo:hi] = -change
@@ -499,7 +512,7 @@
         def job():
             nug_own = jnp.sum(jnp.where(eye, nug_ref[...], 0.0), axis=1, keepdims=True)
             partial[:, lo:hi] = matern(
-                p_l[:, PB:], sq_l[PB:, :], c_r[:, lo:hi], sq_c[:, lo:hi]
+                p_l[PB:, :], sq_l[PB:, :], c_r[:, lo:hi], sq_c[:, lo:hi]
             ) + jnp.where(r * RB + sub == column_ids(lo, hi - lo), nug_own, 0.0)
 
         return job
@@ -514,8 +527,9 @@
     def pieces(lo, hi, size=2 * RB):
         return [(x, min(hi, x + size)) for x in range(lo, hi, size)]
 
+    prepare(0)()
     panel_job(0, 0, RB)()
-    jobs = []
+    jobs = [prepare(i) for i in range(1, NC + 1)]
     for i in range(NC):
         spans = pieces((i if i else 1) * RB, PB) if i == 0 else [(i * RB, (i + 1) * RB)]
         if i:
@@ -526,6 +540,8 @@
     square = big[0:RB, 0:RB]
     for k in range(NC):
         at = k * RB
+        if k == 2:
+            jobs = [prepare_columns(i) for i in range(NC)] + jobs
         if k in extra:
             jobs += [across_job(*x) for x in slices[extra[k][0] : extra[k][1]]]
         if k == NC - 1:
@@ -540,9 +556,9 @@
             beside = stacked(left, right_stack(parts(big[at:nxt, nxt : nxt + RB])), 1)
             p = parts(beside)
             square = big[nxt : nxt + RB, nxt : nxt + RB] - stacked(left_stack(p), right_stack(p))
-            keep(k % 2, nxt, nxt + RB, beside)
+            keep(k, nxt, nxt + RB, beside)
         big[at:nxt, at:nxt] = inverse
-        keep(k % 2, at, nxt, inverse)
+        keep(k, at, nxt, inverse)
         jobs = [row_job(k, left, lo, hi) for lo, hi in pieces(0, at)]
         jobs += [row_job(k, left, lo, hi) for lo, hi in pieces(min(nxt + RB, PB), WIDTH)]
         for i in range(k + 1, NC):
@@ -563,7 +579,7 @@
             schur_ref[:, q, :] = value[:, q * RB - lo : (q + 1) * RB - lo]
 
 
-def factor_and_update(where, blk, col, pan, pnug, nugget, lengthscale):
+def factor_and_update(where, blk, col, pan, pnug, nugget):
     vmem = pl.BlockSpec(memory_space=pltpu.VMEM)
     f32 = jnp.float32
     return pl.pallas_call(
@@ -572,7 +588,7 @@
             jax.ShapeDtypeStruct((RB, NC, RB), f32),
             jax.ShapeDtypeStruct((RB, PB), f32),
         ),
-        in_specs=[pl.BlockSpec(memory_space=pltpu.SMEM)] + [vmem] * 6,
+        in_specs=[pl.BlockSpec(memory_space=pltpu.SMEM)] + [vmem] * 5,
         out_specs=(vmem, vmem),
         scratch_shapes=[
             pltpu.VMEM((WIDTH, F), f32),
@@ -581,7 +597,7 @@
             pltpu.VMEM((WIDTH, 1), f32),
             pltpu.VMEM((1, WIDTH), f32),
             pltpu.VMEM((1, PB), f32),
-            pltpu.VMEM((6 * F, WIDTH), jnp.bfloat16),
+            pltpu.VMEM((WIDTH, 6 * F), jnp.bfloat16),
             pltpu.VMEM((6 * F, WIDTH), jnp.bfloat16),
             pltpu.VMEM((6 * F, PB), jnp.bfloat16),
             pltpu.VMEM((PB, WIDTH), f32),
@@ -589,17 +605,20 @@
             pltpu.VMEM((PB, RB), f32),
             pltpu.VMEM((2, 3, RB, WIDTH), jnp.bfloat16),
             pltpu.VMEM((RB, PB), f32),
+            pltpu.VMEM((2, 3, PB, RB), jnp.bfloat16),
         ],
         compiler_params=pltpu.CompilerParams(vmem_limit_bytes=48 * 1024 * 1024),
         name="factor",
-    )(where, blk, col, pan, pnug, nugget.reshape(1, RB), lengthscale.reshape(1, F))
+    )(where, blk, col, pan, pnug, nugget.reshape(1, RB))
 
 
 def body(telemetry, target, counts, lengthscale, nugget):
-    block_pts, col_packed, pan_packed, pnug = exchange(telemetry, target, counts, nugget)
+    block_pts, col_packed, pan_packed, pnug = exchange(
+        telemetry, target, counts, nugget, lengthscale
+    )
     where = jnp.stack([lax.axis_index("row"), lax.axis_index("col")]).astype(jnp.int32)
     schur_tile, row_lower = factor_and_update(
-        where, block_pts, col_packed, pan_packed, pnug, nugget, lengthscale
+        where, block_pts, col_packed, pan_packed, pnug, nugget
     )
     return (schur_tile.reshape(RB, 1, PB), row_lower)
 

time: 86.5 us -> 85.6 us (0.990)
  no operation moved by 1% of the time
where the time goes in v1:
time: 85.6 us; the launch traced here: 85.4 us
  Pallas kernels  83.3 us (97%)
  between operations  1.31 us (2%)
    pallas_call x1, Pallas kernels, factor_and_update(): pl.pallas_call(factor_kernel, out_shape=(jax.ShapeDtypeStruct((RB, NC, RB...  41.8 us
    pallas_call x1, Pallas kernels, exchange(): pl.pallas_call(exchange_kernel, out_shape=(jax.ShapeDtypeStruct((RB, F),...  41.5 us

profile of v1, /device:TPU:4, one launch (start us, length us, event | category | flops | bytes accessed | tf_op | source)
XLA Modules:
  0.0 85.4 jit_solution(4108739553011691115)
XLA Ops:
  0.6 0.0 copy-start
  1.3 0.1 pad_add_fusion.where_ref
  1.4 0.0 copy-start.1
  1.4 0.0 copy-start.2
  1.4 0.0 copy-start.3
  1.4 0.0 copy-done
  1.4 0.6 copy-done.1
  2.0 0.0 copy-done.2
  2.0 0.0 copy-done.3
  2.1 41.5 %exchange.1 = (f32[128,64]{1,0:T(8,128)S(1)}, f32[64,8,128]{2,1,0:T(8,128)S(1)}, f32[8,8,8,128]{3,2,1,0:T(8,128)S(1)}, f32[8,8,128]{2,1,0:T(8,128)S(1)}) custom-call(f32[1,32,64]{2,1,0:T(8,128)S(1)} %copy-done, s32[1,32]{1,0:T(1,128)S(1)} %copy-done.2, s32[1,1]{1,0:T(1,128)S(6)} %copy.8.cnt_ref, f32[1,128]{1,0:T(1,128)S(1)} %bitcast.5, f32[1,64]{1,0:T(1,128)S(1)} %bitcast.7), custom_call_target="tpu_custom_call" | custom-call | tf_op jit(solution)/shard_map/exchange/pallas_call | solution.py:228
  43.6 41.8 %factor.1 = (f32[128,8,128]{2,1,0:T(8,128)}, f32[128,1024]{1,0:T(8,128)}) custom-call(s32[2]{0:T(128)S(1)} %pad_add_fusion.where_ref, f32[128,64]{1,0:T(8,128)S(1)} %get-tuple-element.8.blk_ref, f32[64,8,128]{2,1,0:T(8,128)S(1)} %get-tuple-element.9.col_ref, f32[8,8,8,128]{3,2,1,0:T(8,128)S(1)} %get-tuple-element.10.pan_ref, ...), custom_call_target="tpu_custom_call" | custom-call | tf_op jit(solution)/shard_map/factor/pallas_call | solution.py:585
Async XLA Ops:
  0.6 0.8 copy-start
  1.4 0.7 copy-start.1
  1.4 0.7 copy-start.2
  1.4 0.7 copy-start.3
